TPU v7x, 1024 devices: a whole 4x4x32 slice. The times are simulated.
1024 devices in a mesh: dp: 64 (over z, core), expert: 16 (over x, y).
Axes of the slice: x: 4, y: 4, z: 32, core: 2. Of those that a mesh axis runs over, the one named last changes fastest.
Arguments:
- out_grad: bfloat16 [49152, 2048], P(('dp', 'expert')), may hold values from -6 to 6
- probs: bfloat16 [49152, 8], P(('dp', 'expert')), may hold values from 0.049804688 to 0.5
- expert_ids: int32 [49152, 8], P(('dp', 'expert')), may hold values from 0 to 15, all different within a row; in each aligned block of 48 rows (0 to 47, 48 to 95, ...) at most 28 rows name the same one
- saved_pre: bfloat16 [458752, 1536], P(('dp', 'expert')), may hold values from -5 to 5
- down_weight: bfloat16 [16, 2048, 768], P('expert'), may hold values from -0.21875 to 0.21875
Outputs:
- grad_down: float32 [16, 2048, 768], P('expert', 'dp')
- grad_pre: bfloat16 [458752, 1536], P(('dp', 'expert'))
- grad_probs: float32 [49152, 8], P(('dp', 'expert'))
Inputs may be any that keep to these rules, and one draw needn't show every extreme that they name: `expert_ids`: each row names 8 different experts; within the 48 tokens of one device no expert is named by more than 28 tokens, a bound that some block reaches of them.
All inputs are finite; a program needn't handle non-finite values.
Results may differ from a plain program's by a relative error of at most 0.007.
Values may be sent and summed in bfloat16 or wider, within the bound.
A program may use at most 64 MiB of HBM per device.

v0:
```python
import jax
import jax.numpy as jnp
from jax import lax
from jax.sharding import PartitionSpec as P


def local(out_grad, probs, expert_ids, saved_pre, down_weight):
    tok_count, top_count = expert_ids.shape
    model_width = out_grad.shape[1]
    hidden_width = saved_pre.shape[1] // 2
    owners = lax.axis_size("expert")
    per_owner = down_weight.shape[0]
    capacity = saved_pre.shape[0] // (per_owner * owners)
    experts_all = per_owner * owners
    onehot = expert_ids[:, :, None] == jnp.arange(experts_all, dtype=jnp.int32)[None, None, :]
    per_token = jnp.sum(onehot.astype(jnp.int32), axis=1)
    before = jnp.cumsum(per_token, axis=0) - per_token
    slot_index = jnp.sum(jnp.where(onehot, before[:, None, :], 0), axis=2)
    owner_of = expert_ids // per_owner
    local_of = expert_ids % per_owner
    target = ((local_of * owners + owner_of) * capacity + slot_index).reshape(-1)
    matches = target[None, :] == jnp.arange(experts_all * capacity, dtype=jnp.int32)[:, None]
    token_match = jnp.sum(
        matches.reshape(experts_all * capacity, tok_count, top_count).astype(jnp.float32), axis=2
    ).astype(jnp.bfloat16)
    routed = jnp.dot(token_match, out_grad, preferred_element_type=jnp.float32).astype(jnp.bfloat16)
    prob_flat = probs.reshape(-1).astype(jnp.float32)
    routed_p = jnp.sum(jnp.where(matches, prob_flat[None, :], 0.0), axis=1).astype(jnp.bfloat16)
    outgoing = routed.reshape(per_owner, owners, capacity, model_width)
    outgoing_p = routed_p.reshape(per_owner, owners, capacity)
    arrived, arrived_p = (
        lax.all_to_all(outgoing, "expert", split_axis=1, concat_axis=1, tiled=True),
        lax.all_to_all(outgoing_p, "expert", split_axis=1, concat_axis=1, tiled=True),
    )
    slot_rows = owners * capacity
    arrived = arrived.reshape(per_owner, slot_rows, model_width)
    weight_row = arrived_p.reshape(per_owner, slot_rows, 1).astype(jnp.float32)
    stored = saved_pre.reshape(per_owner, slot_rows, 2 * hidden_width).astype(jnp.float32)
    gate_pre = stored[..., :hidden_width]
    up_pre = stored[..., hidden_width:]
    sigmoid_gate = jax.nn.sigmoid(gate_pre)
    hidden = (gate_pre * sigmoid_gate * up_pre).astype(jnp.bfloat16)
    scaled = (weight_row * arrived.astype(jnp.float32)).astype(jnp.bfloat16)
    back_proj = jnp.einsum("erd,edh->erh", arrived, down_weight, preferred_element_type=jnp.float32)
    products = jnp.sum(hidden.astype(jnp.float32) * back_proj, axis=2)
    grad_hidden = weight_row * back_proj
    grad_gate = grad_hidden * up_pre * sigmoid_gate * (1.0 + gate_pre * (1.0 - sigmoid_gate))
    grad_up = grad_hidden * gate_pre * sigmoid_gate
    grad_pre = jnp.concatenate([grad_gate, grad_up], axis=2).astype(jnp.bfloat16)
    grad_pre = grad_pre.reshape(per_owner * slot_rows, 2 * hidden_width)
    summed = lax.psum_scatter(
        jnp.einsum("erd,erh->deh", scaled, hidden, preferred_element_type=jnp.float32),
        "dp",
        scatter_dimension=0,
        tiled=True,
    )
    grad_down = jnp.transpose(summed, (1, 0, 2))
    returned = lax.all_to_all(
        products.reshape(per_owner, owners, capacity),
        "expert",
        split_axis=1,
        concat_axis=1,
        tiled=True,
    )
    values = returned.reshape(experts_all * capacity)
    grad_probs = jnp.sum(jnp.where(matches, values[:, None], 0.0), axis=0).reshape(
        tok_count, top_count
    )
    return (grad_down, grad_pre, grad_probs)


def solution(mesh):
    in_specs = (
        P(("dp", "expert"), None),
        P(("dp", "expert"), None),
        P(("dp", "expert"), None),
        P(("dp", "expert"), None),
        P("expert", None, None),
    )
    out_specs = (P("expert", "dp", None), P(("dp", "expert"), None), P(("dp", "expert"), None))
    return jax.shard_map(local, mesh=mesh, in_specs=in_specs, out_specs=out_specs, check_vma=False)
```

profile of v0, /device:TPU:24, one launch (start us, length us, event | category | flops | bytes accessed | tf_op | source)
XLA Modules:
  0.0 554.9 jit_solution(3036184834539643235)
XLA Ops:
  7.2 0.0 copy-start
  7.2 0.9 convert_reduce_fusion.1
  8.0 0.1 copy.40
  8.1 0.1 reduce_window_sum.11
  8.2 0.1 copy.42
  8.3 0.7 select_reduce_fusion.2
  9.0 0.7 multiply_add_fusion
  9.7 0.1 copy.43
  9.8 0.3 convert_reduce_fusion
  10.1 2.8 convolution_convert_fusion
  12.9 3.5 reshape.157
  16.4 17.0 %all-to-all-start.1 = ((bf16[1,16,28,2048]{3,2,0,1:T(8,128)(2,1)}), bf16[1,16,28,2048]{3,2,0,1:T(8,128)(2,1)}, u32[]{:S(2)}, u32[]{:S(2)}) async-start(bf16[1,16,28,2048]{3,2,0,1:T(8,128)(2,1)} %bitcast.55), calls=%async_computation.1 | async-start | bytes 4194304 | tf_op jit(solution)/shard_map/all_to_all | solution.py:32
  33.5 3.2 bitcast_convert_fusion
  36.7 14.7 %all-to-all-done.1 = bf16[1,16,28,2048]{3,2,0,1:T(8,128)(2,1)} async-done(((bf16[1,16,28,2048]{3,2,0,1:T(8,128)(2,1)}), bf16[1,16,28,2048]{3,2,0,1:T(8,128)(2,1)}, u32[]{:S(2)}, u32[]{:S(2)}) %all-to-all-start.1) | async-done | bytes 1835040 | tf_op jit(solution)/shard_map/all_to_all | solution.py:32
  51.3 3.6 reshape.158
  55.0 0.0 copy-done
  55.0 5.2 fusion.4
  60.2 0.7 reshape.160
  60.9 6.3 %all-to-all-start.2 = ((f32[1,16,28]{2,0,1:T(1,128)}), f32[1,16,28]{2,0,1:T(1,128)S(1)}, u32[]{:S(2)}, u32[]{:S(2)}) async-start(f32[1,16,28]{2,0,1:T(1,128)} %reshape.160), calls=%async_computation.2 | async-start | bytes 16384 | tf_op jit(solution)/shard_map/all_to_all | solution.py:58
  67.3 0.1 eq.40
  67.3 0.0 copy-done.1
  67.3 0.1 copy.44
  67.4 0.1 reshape.163
  67.5 5.3 all-to-all-done.2
  72.8 0.5 broadcast.63
  73.3 0.7 reduce.8
  74.0 0.1 broadcast_in_dim.45
  74.1 0.3 select_reduce_fusion
  74.3 0.7 convert_element_type.127
  75.0 5.3 all-to-all-start
  80.4 0.2 all-reduce.3.cloned.1.call-start
  80.6 6.7 %reshape.165 = f32[1,448,1,1,1,1,2048]{6,0,1,5,4,3,2:T(1,128)} reshape(bf16[1,16,28,2048]{3,2,0,1:T(8,128)(2,1)} %all-to-all-done.1) | data formatting | bytes 5505024 | tf_op jit(solution)/shard_map/convert_element_type | solution.py:43
  87.3 0.0 all-to-all-done
  87.3 0.1 reshape.164
  87.4 0.0 copy-start.2
  87.4 4.7 multiply_convert_fusion
  92.1 0.0 copy-done.2
  92.2 4.8 convolution_bitcast_fusion
  96.9 15.9 %copy.48 = f32[2048,1,768]{2,1,0:T(1,128)} copy(f32[2048,1,768]{0,2,1:T(8,128)} %convolution_bitcast_fusion) | data formatting | bytes 12582912 | tf_op jit(solution)/shard_map/erd,erh->deh/transpose | solution.py:52
  112.9 0.0 all-reduce.3.cloned.1.call-update
  112.9 1.3 dynamic-slice
  114.8 0.1 reshape.161
  114.9 0.7 copy.50
  115.6 2.8 fusion.12
  118.4 1.2 pad_maximum_fusion
  119.6 426.9 %all-reduce.3.cloned.1.call-done = f32[2048,1,768]{2,1,0:T(1,128)} async-done(((f32[2048,1,768]{2,1,0:T(1,128)}), f32[2048,1,768]{2,1,0:T(1,128)}) %all-reduce.3.cloned.1.call-update) | async-done | bytes 6291472
  546.5 0.9 dynamic-slice_bitcast_fusion
  547.5 0.6 copy.49
  (3 shorter events, 0.0 us)
Async XLA Ops:
  7.2 47.8 %copy-start = (bf16[1,2048,768]{2,1,0:T(8,128)(2,1)S(1)}, bf16[1,2048,768]{2,1,0:T(8,128)(2,1)}, u32[]{:S(2)}) copy-start(bf16[1,2048,768]{2,1,0:T(8,128)(2,1)} %param.9) | copy-start | bytes 9437188
  16.4 34.9 %all-to-all-start.1 = ((bf16[1,16,28,2048]{3,2,0,1:T(8,128)(2,1)}), bf16[1,16,28,2048]{3,2,0,1:T(8,128)(2,1)}, u32[]{:S(2)}, u32[]{:S(2)}) async-start(bf16[1,16,28,2048]{3,2,0,1:T(8,128)(2,1)} %bitcast.55), calls=%async_computation.1 | async-start | bytes 4194304 | tf_op jit(solution)/shard_map/all_to_all | solution.py:32
  55.0 12.4 %copy-start.1 = (bf16[48,8]{0,1:T(8,128)(2,1)S(1)}, bf16[48,8]{0,1:T(8,128)(2,1)}, u32[]{:S(2)}) copy-start(bf16[48,8]{0,1:T(8,128)(2,1)} %param.6) | copy-start | bytes 2308
  60.9 11.8 %all-to-all-start.2 = ((f32[1,16,28]{2,0,1:T(1,128)}), f32[1,16,28]{2,0,1:T(1,128)S(1)}, u32[]{:S(2)}, u32[]{:S(2)}) async-start(f32[1,16,28]{2,0,1:T(1,128)} %reshape.160), calls=%async_computation.2 | async-start | bytes 16384 | tf_op jit(solution)/shard_map/all_to_all | solution.py:58
  75.0 12.2 %all-to-all-start = ((bf16[1,16,28]{2,0,1:T(2,128)(2,1)}), bf16[1,16,28]{2,0,1:T(2,128)(2,1)S(1)}, u32[]{:S(2)}, u32[]{:S(2)}) async-start(bf16[1,16,28]{2,0,1:T(2,128)(2,1)} %convert_element_type.127), calls=%async_computation | async-start | bytes 16384 | tf_op jit(solution)/shard_map/all_to_all | solution.py:33
  80.4 466.2 %all-reduce.3.cloned.1.call-start = ((), (), s32[]{:S(2)}) async-start(), calls=%async_computation.3 | async-start | bytes 12582912
  87.4 4.8 copy-start.2
Sparse Core Ops, SparseCore 0:
  113.0 433.4 all-reduce.2
where the time goes:
time: 557 us; the launch traced here: 555 us
  waiting for transfers between devices  447 us (80%)
  local copies, waits for them, and re-layouts  35.9 us (6%)
  starting transfers between devices  28.9 us (5%)
  other arithmetic  15.6 us (3%)
  between operations  14.8 us (3%)
  matrix products  12.9 us (2%)
    unnamed x2, waiting for transfers between devices  427 us
    all_to_all x1, starting transfers between devices, local(): lax.all_to_all(outgoing, 'expert', split_axis=1, concat_axis=1, tiled=True)  17 us
    transpose x1, local copies, waits for them, and re-layouts, local(): jnp.einsum('erd,erh->deh', scaled, hidden, preferred_element_type=jnp.flo...  15.9 us
    all_to_all x1, waiting for transfers between devices, local(): lax.all_to_all(outgoing, 'expert', split_axis=1, concat_axis=1, tiled=True)  14.7 us
  transfers between devices with their start and end apart: 4, of which 3 were waited for; matrix products, arithmetic and copies ran while one was open for 3% of the time, Pallas kernels for 0%

commit v1 on v0

v1 whole, which is shorter than its diff:
```python
import jax
import jax.numpy as jnp
from jax import lax
from jax.experimental import pallas as pl
from jax.experimental.pallas import tpu as pltpu
from jax.sharding import PartitionSpec as P

MESH = pl.DeviceIdType.MESH
F32, BF16 = jnp.float32, jnp.bfloat16
SIDE = 4
OWNERS = 16
CHUNKS = 8
WIDTH = 256
HALF = 128
STEPS = 16
CHIPS = 32
SHARE = 32
SUBS = 2


def div(a, b):
    return lax.div(jnp.int32(a), jnp.int32(b))


def rem(a, b):
    return lax.rem(jnp.int32(a), jnp.int32(b))


def kernel(
    grad_hbm, probs_ref, ids_ref, stored_hbm, weight_hbm,
    down_ref, pre_hbm, gprobs_ref,
    g, w, stored, hidden, d_gate, d_up, back, routed_all, pre,
    pick, prob_col, cols, slot_tab, meta_out, meta_in, prod_out, prod_in,
    part, part_in, acc_out, acc_in,
    sem_g, sem_w, sem_stored, sem_pre, gs, gr, ms, mr, rs, rr, ss, sr, zs, zr,
):
    tok, top = ids_ref.shape
    rows = stored_hbm.shape[0]
    hid_n = weight_hbm.shape[2]
    cap = rows // OWNERS
    dp = lax.axis_index("dp")
    me = lax.axis_index("expert")
    z, core = div(dp, 2), rem(dp, 2)
    x, y = div(me, SIDE), rem(me, SIDE)
    odd = rem(z, 2)
    first_group = div(z + STEPS, 2)
    n_groups = 2 * CHUNKS
    up_z = (rem(z + 1, CHIPS) * 2 + core, me)
    down_z = (rem(z + CHIPS - 1, CHIPS) * 2 + core, me)
    sibling = (z * 2 + 1 - core, me)

    def own_coords(i):
        par = rem(i, 2)
        return par, y * (1 - par) + x * par, x * (1 - par) + y * par

    def group_of(i, half):
        par = rem(i, 2)
        start = (1 - par) * i - par * (i + 1)
        return rem(first_group + start + half + 2 * n_groups, n_groups)

    def load_g(i, half):
        _, u, v = own_coords(i)
        at = pl.multiple_of(group_of(i, half) * HALF, HALF)
        return pltpu.make_async_copy(
            grad_hbm.at[:, pl.ds(at, HALF)],
            g.at[i, u, v, :, pl.ds(half * HALF, HALF)],
            sem_g.at[i, half],
        )

    def load_w(i, half):
        at = pl.multiple_of(group_of(i, half) * HALF, HALF)
        return pltpu.make_async_copy(
            weight_hbm.at[0, pl.ds(at, HALF), :],
            w.at[i, pl.ds(half * HALF, HALF), :],
            sem_w.at[i, half],
        )

    for i in range(CHUNKS):
        for half in range(2):
            load_g(i, half).start()
    load_stored = pltpu.make_async_copy(stored_hbm, stored, sem_stored)
    load_stored.start()
    for i in range(CHUNKS):
        for half in range(2):
            load_w(i, half).start()

    barrier = pltpu.get_barrier_semaphore()

    def greet(j, carry):
        pl.semaphore_signal(barrier, inc=1, device_id=(dp, rem(me + j, OWNERS)), device_id_type=MESH)
        return carry

    for target in (up_z, down_z, sibling):
        pl.semaphore_signal(barrier, inc=1, device_id=target, device_id_type=MESH)
    lax.fori_loop(1, OWNERS, greet, 0)

    lane = lax.broadcasted_iota(jnp.int32, (tok, HALF), 1)
    chosen = jnp.zeros((tok, HALF), F32)
    prob = jnp.zeros((tok, HALF), F32)
    for k in range(top):
        hit = ids_ref[:, k : k + 1] == lane
        chosen = chosen + jnp.where(hit, 1.0, 0.0)
        prob = prob + jnp.where(hit, probs_ref[:, k : k + 1].astype(F32), 0.0)
    lower = (
        lax.broadcasted_iota(jnp.int32, (tok, tok), 0) > lax.broadcasted_iota(jnp.int32, (tok, tok), 1)
    )
    before = jnp.dot(
        jnp.where(lower, 1.0, 0.0).astype(BF16), chosen.astype(BF16), preferred_element_type=F32
    )
    slots = jnp.where(chosen > 0.0, before, -1.0)
    slot_tab[...] = slots
    fill = jnp.zeros((HALF - tok, HALF), F32)
    slots_t = jnp.concatenate([slots, fill - 1.0], axis=0).T
    prob_t = jnp.concatenate([prob, fill], axis=0).T
    sub8 = lax.broadcasted_iota(jnp.int32, (8, HALF), 0)
    for e in range(OWNERS):
        meta_out[e] = jnp.where(
            sub8 == 0,
            jnp.broadcast_to(slots_t[e : e + 1], (8, HALF)),
            jnp.broadcast_to(prob_t[e : e + 1], (8, HALF)),
        )
    meta_in[me] = meta_out[me]

    pl.semaphore_wait(barrier, OWNERS - 1 + 3)

    def move(i, k):
        par, u, v = own_coords(i)
        turn = rem(div(i, 2), 2)
        if k < 3:
            step = (1, SIDE - 1, None)[k]
            if k == 2:
                source, step = rem(v + SIDE - 1 + 2 * turn, SIDE), SIDE + 1 - 2 * turn
            else:
                source = v
            block = g.at[i, u, source]
            uu, vv = u, rem(v + step, SIDE)
        else:
            step = (1, SIDE - 1, None)[k - 3]
            if k == 5:
                source, step = rem(u + SIDE - 1 + 2 * turn, SIDE), SIDE + 1 - 2 * turn
            else:
                source = u
            block = g.at[i, source]
            uu, vv = rem(u + step, SIDE), v
        xx = vv * (1 - par) + uu * par
        yy = uu * (1 - par) + vv * par
        return pltpu.make_async_remote_copy(
            src_ref=block, dst_ref=block, send_sem=gs.at[i, k], recv_sem=gr.at[i, k],
            device_id=(dp, xx * SIDE + yy), device_id_type=MESH,
        )

    def stage_a(i):
        load_g(i, 0).wait()
        load_g(i, 1).wait()
        move(i, 0).start()
        move(i, 1).start()

    def stage_b(i):
        move(i, 0).wait_recv()
        move(i, 1).wait_recv()
        move(i, 2).start()

    def stage_c(i):
        move(i, 2).wait_recv()
        move(i, 3).start()
        move(i, 4).start()

    def stage_d(i):
        move(i, 3).wait_recv()
        move(i, 4).wait_recv()
        move(i, 5).start()

    def meta_copy(j):
        other = rem(me + j, OWNERS)
        return pltpu.make_async_remote_copy(
            src_ref=meta_out.at[other], dst_ref=meta_in.at[me], send_sem=ms.at[j], recv_sem=mr.at[j],
            device_id=(dp, other), device_id_type=MESH,
        )

    def prod_copy(j):
        other = rem(me + j, OWNERS)
        return pltpu.make_async_remote_copy(
            src_ref=prod_out.at[other], dst_ref=prod_in.at[me], send_sem=rs.at[j], recv_sem=rr.at[j],
            device_id=(dp, other), device_id_type=MESH,
        )

    def for_peers(act):
        def body(j, carry):
            act(j)
            return carry

        lax.fori_loop(1, OWNERS, body, 0)

    def gates(b, size):
        at = pl.ds(b * size, size)
        a = stored[at, :hid_n].astype(F32)
        up = stored[at, hid_n:].astype(F32)
        sg = jax.nn.sigmoid(a)
        act = a * sg
        hidden[at, :] = (act * up).astype(BF16)
        d_gate[at, :] = up * sg * (1.0 + a * (1.0 - sg))
        d_up[at, :] = act

    def build_pick():
        sub16 = lax.broadcasted_iota(jnp.int32, (HALF, HALF), 0)
        slot_rows = jnp.full((HALF, HALF), -1.0, F32)
        prob_rows = jnp.zeros((HALF, HALF), F32)
        for s in range(OWNERS):
            slot_rows = jnp.where(sub16 == s, jnp.broadcast_to(meta_in[s, 0:1, :], (HALF, HALF)), slot_rows)
            prob_rows = jnp.where(sub16 == s, jnp.broadcast_to(meta_in[s, 1:2, :], (HALF, HALF)), prob_rows)
        slot_cols = slot_rows.T
        prob_cols = prob_rows.T
        for par in range(2):
            for block in range(OWNERS):
                outer, inner = block // SIDE, block % SIDE
                s = inner * SIDE + outer if par == 0 else block
                col = slot_cols[0:tok, s : s + 1]
                place = jnp.where(col >= 0.0, col + float(cap * s), -1.0)
                cols[block * tok : (block + 1) * tok, :] = jnp.where(
                    lane == 0,
                    jnp.broadcast_to(place, (tok, HALF)),
                    jnp.broadcast_to(prob_cols[0:tok, s : s + 1], (tok, HALF)),
                )
            flat = cols[...].T
            place_row = flat[0:1, :].astype(jnp.int32)
            n_tok = OWNERS * tok
            match = jnp.broadcast_to(place_row, (rows, n_tok)) == lax.broadcasted_iota(jnp.int32, (rows, n_tok), 0)
            pick[par] = jnp.where(match, 1.0, 0.0).astype(BF16)
            if par == 0:
                total = jnp.sum(
                    jnp.where(match, jnp.broadcast_to(flat[1:2, :], (rows, n_tok)), 0.0), axis=1, keepdims=True
                )
                prob_col[...] = jnp.broadcast_to(total, (rows, HALF))

    def sib_copy(i):
        at = pl.ds(4 * i, 4)
        return pltpu.make_async_remote_copy(
            src_ref=part.at[at, 1 - core], dst_ref=part_in.at[at], send_sem=ss.at[i], recv_sem=sr.at[i],
            device_id=sibling, device_id_type=MESH,
        )

    def stage_e(i):
        move(i, 5).wait_recv()
        tokens = g[i].reshape(OWNERS * tok, WIDTH)
        routed = jnp.dot(pick[rem(i, 2)], tokens, preferred_element_type=F32)
        routed_all[i] = routed.astype(BF16)
        weight_row = jnp.concatenate([prob_col[...], prob_col[...]], axis=1)
        scaled = (weight_row * routed).astype(BF16)
        summed = lax.dot_general(
            scaled, hidden[...], (((0,), (0,)), ((), ())), preferred_element_type=F32
        )
        part[pl.ds(4 * i, 4)] = summed.astype(BF16).reshape(4, 2, SUBS, SHARE // SUBS, hid_n)
        sib_copy(i).start()

    def add_back(i):
        load_w(i, 0).wait()
        load_w(i, 1).wait()
        back[...] += jnp.dot(routed_all[i], w[i], preferred_element_type=F32)

    def chip_slot(off):
        at = off + STEPS
        m = rem(div(at, 2), n_groups)
        high = div(m, CHUNKS)
        chunk = (1 - high) * (7 - 2 * div(m, 2)) + high * 2 * div(m - CHUNKS * high, 2)
        return 4 * chunk + 2 * rem(m, 2) + rem(at, 2)

    def hop(way, s, k):
        return pltpu.make_async_remote_copy(
            src_ref=acc_out.at[way, s, k], dst_ref=acc_in.at[way, s + 1, k],
            send_sem=zs.at[way, s, k], recv_sem=zr.at[way, s, k],
            device_id=(up_z, down_z)[way], device_id_type=MESH,
        )

    def local_sum(slot, k):
        return part[slot, core, k].astype(F32) + part_in[slot, k].astype(F32)

    def ring_step(s, ways=(0, 1), first=None):
        for k in range(SUBS):
            for way in ways:
                slot = chip_slot(odd - s) if way == 0 else chip_slot(odd + 1 + s)

                def arrive():
                    hop(way, s - 1, k).wait_recv()

                if first is None:
                    pl.when(s > 0)(arrive)
                else:
                    arrive()
                acc_out[way, s, k] = (acc_in[way, s, k].astype(F32) + local_sum(slot, k)).astype(BF16)
                hop(way, s, k).start()

    for_peers(lambda j: meta_copy(j).start())
    stage_a(0)
    stage_a(1)
    load_stored.wait()
    quarter = rows // 4
    gates(0, quarter)
    stage_b(0)
    stage_b(1)
    stage_a(2)
    gates(1, quarter)
    stage_c(0)
    stage_c(1)
    stage_b(2)
    stage_a(3)
    for_peers(lambda j: meta_copy(j).wait_recv())
    build_pick()
    stage_d(0)
    stage_d(1)
    stage_c(2)
    stage_b(3)
    stage_a(4)
    gates(2, quarter)
    gates(3, quarter)
    back[...] = jnp.zeros_like(back)
    acc_in[0, 0] = jnp.zeros(acc_in.shape[2:], BF16)
    acc_in[1, 0] = jnp.zeros(acc_in.shape[2:], BF16)
    stage_d(2)
    stage_c(3)
    stage_b(4)
    stage_a(5)

    def pair(i, carry):
        stage_e(i)
        return carry

    lax.fori_loop(0, 2, pair, 0)
    sib_copy(0).wait_recv()

    def turn_body(j, carry):
        sib_copy(j + 1).wait_recv()
        ring_step(2 * j)

        @pl.when(j < 5)
        def _():
            stage_d(j + 3)

        @pl.when(j < 4)
        def _():
            stage_c(j + 4)

        @pl.when(j < 3)
        def _():
            stage_b(j + 5)

        @pl.when(j < 2)
        def _():
            stage_a(j + 6)

        stage_e(j + 2)
        ring_step(2 * j + 1)
        add_back(j)
        return carry

    lax.fori_loop(0, 6, turn_body, 0)
    sib_copy(7).wait_recv()
    ring_step(12, first=False)
    add_back(6)
    add_back(7)
    ring_step(13, first=False)

    products = jnp.sum(hidden[...].astype(F32) * back[...], axis=1, keepdims=True)
    row_at = lax.broadcasted_iota(jnp.int32, (rows, HALF), 0).astype(F32)
    row_slot = row_at - float(cap) * jnp.floor((row_at + 0.5) * (1.0 / cap))
    lane_at = lax.broadcasted_iota(jnp.int32, (rows, HALF), 1).astype(F32)
    spread = jnp.where(lane_at == row_slot, jnp.broadcast_to(products, (rows, HALF)), 0.0)
    src_at = jnp.floor((lax.broadcasted_iota(jnp.int32, (OWNERS, rows), 1).astype(F32) + 0.5) * (1.0 / cap))
    gather = jnp.where(src_at == lax.broadcasted_iota(jnp.int32, (OWNERS, rows), 0).astype(F32), 1.0, 0.0)
    by_source = jnp.dot(gather, spread, preferred_element_type=F32, precision=lax.Precision.HIGHEST)
    for s in range(OWNERS):
        prod_out[s] = jnp.broadcast_to(by_source[s : s + 1], (8, HALF))
    prod_in[me] = prod_out[me]
    for_peers(lambda j: prod_copy(j).start())

    ring_step(14, first=False)

    def finish_rows(b, size):
        at = pl.ds(b * size, size)
        scale = jnp.concatenate([prob_col[at, :]] * (hid_n // HALF), axis=1)
        grad = scale * back[at, :]
        pre[at, :hid_n] = (grad * d_gate[at, :]).astype(BF16)
        pre[at, hid_n:] = (grad * d_up[at, :]).astype(BF16)

    def store_pre(b, size):
        at = pl.ds(b * size, size)
        return pltpu.make_async_copy(pre.at[at], pre_hbm.at[at], sem_pre.at[b])

    half_rows = rows // 2
    finish_rows(0, half_rows)
    store_pre(0, half_rows).start()
    ring_step(15, ways=(0,), first=False)
    finish_rows(1, half_rows)
    store_pre(1, half_rows).start()

    for_peers(lambda j: prod_copy(j).wait_recv())
    lane_f = lane.astype(F32)
    per_owner = jnp.zeros((tok, HALF), F32)
    for e in range(OWNERS):
        hit = jnp.broadcast_to(slot_tab[:, e : e + 1], (tok, HALF)) == lane_f
        value = jnp.sum(
            jnp.where(hit, jnp.broadcast_to(prod_in[e, 0:1, :], (tok, HALF)), 0.0), axis=1, keepdims=True
        )
        per_owner = jnp.where(lane == e, jnp.broadcast_to(value, (tok, HALF)), per_owner)
    lane_top = lax.broadcasted_iota(jnp.int32, (tok, top), 1)
    result = jnp.zeros((tok, top), F32)
    for k in range(top):
        value = jnp.sum(jnp.where(ids_ref[:, k : k + 1] == lane, per_owner, 0.0), axis=1, keepdims=True)
        result = jnp.where(lane_top == k, jnp.broadcast_to(value, (tok, top)), result)
    gprobs_ref[...] = result

    own = chip_slot(odd - STEPS)
    piece = SHARE // SUBS
    for k in range(SUBS):
        hop(1, STEPS - 2, k).wait_recv()
        hop(0, STEPS - 1, k).wait_recv()
        down_ref[0, k * piece : (k + 1) * piece, :] = (
            acc_in[0, STEPS, k].astype(F32) + acc_in[1, STEPS - 1, k].astype(F32) + local_sum(own, k)
        )

    def drain(i, carry):
        for k in range(6):
            move(i, k).wait_send()
        sib_copy(i).wait_send()
        return carry

    lax.fori_loop(0, CHUNKS, drain, 0)
    for_peers(lambda j: meta_copy(j).wait_send())
    for_peers(lambda j: prod_copy(j).wait_send())

    def drain_ring(s, carry):
        for k in range(SUBS):
            for way in range(2):
                hop(way, s, k).wait_send()
        return carry

    lax.fori_loop(0, STEPS - 1, drain_ring, 0)
    for k in range(SUBS):
        hop(0, STEPS - 1, k).wait_send()
    store_pre(0, half_rows).wait()
    store_pre(1, half_rows).wait()


def local(out_grad, probs, expert_ids, saved_pre, down_weight):
    tok, top = expert_ids.shape
    rows, pre_n = saved_pre.shape
    hid_n = pre_n // 2
    piece = SHARE // SUBS
    dma = pltpu.SemaphoreType.DMA
    scratch = [
        pltpu.VMEM((CHUNKS, SIDE, SIDE, tok, WIDTH), BF16),
        pltpu.VMEM((CHUNKS, WIDTH, hid_n), BF16),
        pltpu.VMEM((rows, pre_n), BF16),
        pltpu.VMEM((rows, hid_n), BF16),
        pltpu.VMEM((rows, hid_n), F32),
        pltpu.VMEM((rows, hid_n), F32),
        pltpu.VMEM((rows, hid_n), F32),
        pltpu.VMEM((CHUNKS, rows, WIDTH), BF16),
        pltpu.VMEM((rows, pre_n), BF16),
        pltpu.VMEM((2, rows, OWNERS * tok), BF16),
        pltpu.VMEM((rows, HALF), F32),
        pltpu.VMEM((OWNERS * tok, HALF), F32),
        pltpu.VMEM((tok, HALF), F32),
        pltpu.VMEM((OWNERS, 8, HALF), F32),
        pltpu.VMEM((OWNERS, 8, HALF), F32),
        pltpu.VMEM((OWNERS, 8, HALF), F32),
        pltpu.VMEM((OWNERS, 8, HALF), F32),
        pltpu.VMEM((CHIPS, 2, SUBS, piece, hid_n), BF16),
        pltpu.VMEM((CHIPS, SUBS, piece, hid_n), BF16),
        pltpu.VMEM((2, STEPS, SUBS, piece, hid_n), BF16),
        pltpu.VMEM((2, STEPS + 1, SUBS, piece, hid_n), BF16),
        dma((CHUNKS, 2)), dma((CHUNKS, 2)), dma, dma((2,)),
        dma((CHUNKS, 6)), dma((CHUNKS, 6)),
        dma((OWNERS,)), dma((OWNERS,)), dma((OWNERS,)), dma((OWNERS,)),
        dma((CHUNKS,)), dma((CHUNKS,)),
        dma((2, STEPS, SUBS)), dma((2, STEPS, SUBS)),
    ]
    hbm = pl.BlockSpec(memory_space=pl.ANY)
    vmem = pl.BlockSpec(memory_space=pltpu.VMEM)
    return pl.pallas_call(
        kernel,
        out_shape=(
            jax.ShapeDtypeStruct((1, SHARE, hid_n), F32),
            jax.ShapeDtypeStruct((rows, pre_n), BF16),
            jax.ShapeDtypeStruct((tok, top), F32),
        ),
        in_specs=[hbm, vmem, vmem, hbm, hbm],
        out_specs=(vmem, hbm, vmem),
        scratch_shapes=scratch,
        compiler_params=pltpu.CompilerParams(
            collective_id=0, has_side_effects=True, vmem_limit_bytes=56 * 1024 * 1024
        ),
    )(out_grad, probs, expert_ids, saved_pre, down_weight)


def solution(mesh):
    in_specs = (
        P(("dp", "expert"), None),
        P(("dp", "expert"), None),
        P(("dp", "expert"), None),
        P(("dp", "expert"), None),
        P("expert", None, None),
    )
    out_specs = (P("expert", "dp", None), P(("dp", "expert"), None), P(("dp", "expert"), None))
    return jax.shard_map(local, mesh=mesh, in_specs=in_specs, out_specs=out_specs, check_vma=False)
```

time: 557 us -> 106 us (0.19)
  waiting for transfers between devices: 447 us -> 0 us
  Pallas kernels: 0 us -> 96.6 us
  starting transfers between devices: 28.9 us -> 0 us
  local copies, waits for them, and re-layouts: 35.9 us -> 8.18 us
  other arithmetic: 15.6 us -> 0 us
  between operations: 14.8 us -> 0.64 us
  matrix products: 12.9 us -> 0 us
    unnamed x2 -> x0, waiting for transfers between devices: 427 us -> none
    pallas_call x0 -> x1, Pallas kernels: none -> 96.6 us  [local(): pl.pallas_call(kernel, out_shape=(jax.ShapeDtypeStruct((1, SHARE, hid_n),...]
    all_to_all x3 -> x0, starting transfers between devices: 28.7 us -> none  [the longest x1 17 us: local(): lax.all_to_all(outgoing, 'expert', split_axis=1, concat_axis=1, tiled=True)]
    all_to_all x3 -> x0, waiting for transfers between devices: 19.9 us -> none  [the longest x1 14.7 us: local(): lax.all_to_all(outgoing, 'expert', split_axis=1, concat_axis=1, tiled=True)]
    transpose x2 -> x0, local copies, waits for them, and re-layouts: 16.8 us -> none  [the longest x1 15.9 us: local(): jnp.einsum('erd,erh->deh', scaled, hidden, preferred_element_type=jnp.flo...]
    dot_general x3 -> x0, matrix products: 12.9 us -> none  [the longest x1 5.25 us: local(): jnp.einsum('erd,edh->erh', arrived, down_weight, preferred_element_type=j...]
    convert_element_type x3 -> x0, other arithmetic: 7.98 us -> none  [the longest x1 4.73 us: local(): scaled = (weight_row * arrived.astype(jnp.float32)).astype(jnp.bfloat16)]
    convert_element_type x5 -> x0, local copies, waits for them, and re-layouts: 7.63 us -> none  [the longest x1 6.67 us: local(): scaled = (weight_row * arrived.astype(jnp.float32)).astype(jnp.bfloat16)]
  transfers between devices with their start and end apart: 4 -> 0, of which waited for: 3 -> 0; matrix products, arithmetic and copies ran while one was open for 3% -> 0% of each run, Pallas kernels for 0% -> 0%
where the time goes in v1:
time: 106 us; the launch traced here: 105 us
  Pallas kernels  96.6 us (91%)
  local copies, waits for them, and re-layouts  8.18 us (8%)
    pallas_call x1, Pallas kernels, local(): pl.pallas_call(kernel, out_shape=(jax.ShapeDtypeStruct((1, SHARE, hid_n),...  96.6 us
    unnamed x4, local copies, waits for them, and re-layouts  6.78 us

profile of v1, /device:TPU:24, one launch (start us, length us, event | category | flops | bytes accessed | tf_op | source)
XLA Modules:
  0.0 105.4 jit_solution(2687178682519552268)
XLA Ops:
  0.6 1.4 %copy.8.probs_ref = bf16[48,8]{1,0:T(8,128)(2,1)} copy(bf16[48,8]{0,1:T(8,128)(2,1)} %param.6) | data formatting | bytes 1536 | tf_op args[1]
  2.0 1.4 %copy.9.ids_ref = s32[48,8]{1,0:T(8,128)} copy(s32[48,8]{0,1:T(8,128)} %param.7) | data formatting | bytes 3072 | tf_op args[2]
  3.4 96.6 %shard_map.76 = (f32[1,32,768]{2,1,0:T(8,128)}, bf16[448,1536]{1,0:T(8,128)(2,1)}, f32[48,8]{1,0:T(8,128)}) custom-call(bf16[48,2048]{1,0:T(8,128)(2,1)} %grad_hbm.1, bf16[48,8]{1,0:T(8,128)(2,1)} %copy.8.probs_ref, s32[48,8]{1,0:T(8,128)} %copy.9.ids_ref, bf16[448,1536]{1,0:T(8,128)(2,1)} %stored_hbm.1, bf16[1,2048,768]{2,1,0:T(8,128)(2,1)} %weight_hbm.1), custom_call_target="tpu_custom_call" | custom-call | tf_op jit(solution)/shard_map/pallas_call | solution.py:479
  99.9 1.4 %copy.10 = f32[48,8]{0,1:T(8,128)} copy(f32[48,8]{1,0:T(8,128)} %get-tuple-element.5) | data formatting | bytes 3072 | tf_op jit(solution)/shard_map/pallas_call | solution.py:479
  101.3 1.5 %copy.13 = f32[1,32,768]{2,1,0:T(8,128)} copy(f32[1,32,768]{2,1,0:T(8,128)} %get-tuple-element.9) | data formatting | bytes 196608
  102.9 2.5 %copy.14 = bf16[448,1536]{1,0:T(8,128)(2,1)} copy(bf16[448,1536]{1,0:T(8,128)(2,1)} %get-tuple-element.10) | data formatting | bytes 2752512

commit v2 on v1

v2 whole, which is shorter than its diff:
```python
import jax
import jax.numpy as jnp
from jax import lax
from jax.experimental import pallas as pl
from jax.experimental.pallas import tpu as pltpu
from jax.sharding import PartitionSpec as P

MESH = pl.DeviceIdType.MESH
F32, BF16 = jnp.float32, jnp.bfloat16
PAD = 32
OWNERS = 16
CHUNKS = 8
WIDTH = 256
HALF = 128
REACH = 16
STEPS = 8
CHIPS = 32
SHARE = 32
SUBS = 2


def div(a, b):
    return lax.div(jnp.int32(a), jnp.int32(b))


def rem(a, b):
    return lax.rem(jnp.int32(a), jnp.int32(b))


def kernel(
    grad_hbm, probs_ref, ids_ref, stored_hbm, weight_hbm,
    down_ref, pre_hbm, gprobs_ref,
    own_g, w, stored, hidden, d_gate, d_up, back, routed_all, pre,
    select, rows_out, rows_in, prob_out, prob_in, compact, prob_col,
    prod_out, prod_in, part, part_in, acc_out, acc_in, leaf_out, leaf_in,
    sem_g, sem_w, sem_stored, sem_pre, gs, gr, ps, pr, rs, rr, ss, sr, zs, zr, ls, lr,
):
    top, tok = ids_ref.shape
    rows = stored_hbm.shape[0]
    hid_n = weight_hbm.shape[2]
    cap = rows // OWNERS
    dp = lax.axis_index("dp")
    me = lax.axis_index("expert")
    z, core = div(dp, 2), rem(dp, 2)
    odd = rem(z, 2)
    first_group = div(z + REACH, 2)
    n_groups = 2 * CHUNKS
    near = [(rem(z + by, CHIPS) * 2 + core, me) for by in (1, CHIPS - 1)]
    far = [(rem(z + by, CHIPS) * 2 + core, me) for by in (2, CHIPS - 2)]
    sibling = (z * 2 + 1 - core, me)

    barrier = pltpu.get_barrier_semaphore()

    def greet(j, carry):
        pl.semaphore_signal(barrier, inc=1, device_id=(dp, rem(me + j, OWNERS)), device_id_type=MESH)
        return carry

    for target in (*near, *far, sibling):
        pl.semaphore_signal(barrier, inc=1, device_id=target, device_id_type=MESH)
    lax.fori_loop(1, OWNERS, greet, 0)

    def group_of(i, half):
        par = rem(i, 2)
        start = (1 - par) * i - par * (i + 1)
        return rem(first_group + start + half + 2 * n_groups, n_groups)

    def load_g(i, half):
        at = pl.multiple_of(group_of(i, half) * HALF, HALF)
        return pltpu.make_async_copy(
            grad_hbm.at[:, pl.ds(at, HALF)], own_g.at[i, :, pl.ds(half * HALF, HALF)], sem_g.at[i, half]
        )

    def load_w(i, half):
        at = pl.multiple_of(group_of(i, half) * HALF, HALF)
        return pltpu.make_async_copy(
            weight_hbm.at[0, pl.ds(at, HALF), :], w.at[i, pl.ds(half * HALF, HALF), :], sem_w.at[i, half]
        )

    for i in range(CHUNKS):
        for half in range(2):
            load_g(i, half).start()
    load_stored = pltpu.make_async_copy(stored_hbm, stored, sem_stored)
    load_stored.start()
    for i in range(CHUNKS):
        for half in range(2):
            load_w(i, half).start()

    ids = ids_ref[...]
    owner = lax.broadcasted_iota(jnp.int32, (OWNERS, tok), 0)
    chosen = jnp.zeros((OWNERS, tok), F32)
    prob = jnp.zeros((OWNERS, tok), F32)
    probs = probs_ref[...].astype(F32)
    for k in range(top):
        hit = jnp.broadcast_to(ids[k : k + 1], (OWNERS, tok)) == owner
        chosen = chosen + jnp.where(hit, 1.0, 0.0)
        prob = prob + jnp.where(hit, jnp.broadcast_to(probs[k : k + 1], (OWNERS, tok)), 0.0)
    earlier = (
        lax.broadcasted_iota(jnp.int32, (tok, tok), 0) < lax.broadcasted_iota(jnp.int32, (tok, tok), 1)
    )
    before = jnp.dot(
        chosen.astype(BF16), jnp.where(earlier, 1.0, 0.0).astype(BF16), preferred_element_type=F32
    )
    slots = jnp.where(chosen > 0.0, before, -1.0)
    slot_at = lax.broadcasted_iota(jnp.int32, (PAD, tok), 0).astype(F32)
    for e in range(OWNERS):
        match = jnp.broadcast_to(slots[e : e + 1], (PAD, tok)) == slot_at
        select[e * PAD : (e + 1) * PAD, :] = jnp.where(match, 1.0, 0.0).astype(BF16)
        filled = jnp.sum(
            jnp.where(match, jnp.broadcast_to(prob[e : e + 1], (PAD, tok)), 0.0), axis=1, keepdims=True
        )
        prob_out[e] = jnp.broadcast_to(filled, (PAD, HALF)).astype(BF16)

    def pick_rows(i):
        load_g(i, 0).wait()
        load_g(i, 1).wait()
        picked = jnp.dot(select[...], own_g[i], preferred_element_type=F32)
        rows_out[i] = picked.astype(BF16).reshape(OWNERS, PAD, WIDTH)
        rows_in[i, me] = rows_out[i, me]

    pick_rows(0)
    prob_in[me] = prob_out[me]
    pl.semaphore_wait(barrier, OWNERS - 1 + 5)

    def row_copy(i, j):
        other = rem(me + j, OWNERS)
        return pltpu.make_async_remote_copy(
            src_ref=rows_out.at[i, other], dst_ref=rows_in.at[i, me], send_sem=gs.at[i, j], recv_sem=gr.at[i, j],
            device_id=(dp, other), device_id_type=MESH,
        )

    def prob_copy(j):
        other = rem(me + j, OWNERS)
        return pltpu.make_async_remote_copy(
            src_ref=prob_out.at[other], dst_ref=prob_in.at[me], send_sem=ps.at[j], recv_sem=pr.at[j],
            device_id=(dp, other), device_id_type=MESH,
        )

    def prod_copy(j):
        other = rem(me + j, OWNERS)
        return pltpu.make_async_remote_copy(
            src_ref=prod_out.at[other], dst_ref=prod_in.at[me], send_sem=rs.at[j], recv_sem=rr.at[j],
            device_id=(dp, other), device_id_type=MESH,
        )

    def for_peers(act):
        def body(j, carry):
            act(j)
            return carry

        lax.fori_loop(1, OWNERS, body, 0)

    def send_rows(i):
        for_peers(lambda j: row_copy(i, j).start())

    def gates(b, size):
        at = pl.ds(b * size, size)
        a = stored[at, :hid_n].astype(F32)
        up = stored[at, hid_n:].astype(F32)
        sg = jax.nn.sigmoid(a)
        act = a * sg
        hidden[at, :] = (act * up).astype(BF16)
        d_gate[at, :] = up * sg * (1.0 + a * (1.0 - sg))
        d_up[at, :] = act

    def sib_copy(i):
        at = pl.ds(4 * i, 4)
        return pltpu.make_async_remote_copy(
            src_ref=part.at[at, 1 - core], dst_ref=part_in.at[at], send_sem=ss.at[i], recv_sem=sr.at[i],
            device_id=sibling, device_id_type=MESH,
        )

    def stage_e(i):
        for_peers(lambda j: row_copy(i, j).wait_recv())
        arrived = rows_in[i].reshape(OWNERS * PAD, WIDTH)
        routed = jnp.dot(compact[...], arrived, preferred_element_type=F32)
        routed_all[i] = routed.astype(BF16)
        weight_row = jnp.concatenate([prob_col[...], prob_col[...]], axis=1)
        scaled = (weight_row * routed).astype(BF16)
        summed = lax.dot_general(
            scaled, hidden[...], (((0,), (0,)), ((), ())), preferred_element_type=F32
        )
        part[pl.ds(4 * i, 4)] = summed.astype(BF16).reshape(4, 2, SUBS, SHARE // SUBS, hid_n)
        sib_copy(i).start()

    def add_back(i):
        load_w(i, 0).wait()
        load_w(i, 1).wait()
        back[...] += jnp.dot(routed_all[i], w[i], preferred_element_type=F32)

    def chip_slot(off):
        at = off + REACH
        m = rem(div(at, 2), n_groups)
        high = div(m, CHUNKS)
        chunk = (1 - high) * (7 - 2 * div(m, 2)) + high * 2 * div(m - CHUNKS * high, 2)
        return 4 * chunk + 2 * rem(m, 2) + rem(at, 2)

    def hop(way, t, k):
        return pltpu.make_async_remote_copy(
            src_ref=acc_out.at[way, t, k], dst_ref=acc_in.at[way, t + 1, k],
            send_sem=zs.at[way, t, k], recv_sem=zr.at[way, t, k],
            device_id=far[way], device_id_type=MESH,
        )

    def leaf(way, t):
        return pltpu.make_async_remote_copy(
            src_ref=leaf_out.at[way, t], dst_ref=leaf_in.at[way, t + 1],
            send_sem=ls.at[way, t], recv_sem=lr.at[way, t],
            device_id=near[way], device_id_type=MESH,
        )

    def local_sum(slot, k):
        return part[slot, core, k].astype(F32) + part_in[slot, k].astype(F32)

    def guarded(condition, act):
        if isinstance(condition, bool):
            if condition:
                act()
        else:
            pl.when(condition)(act)

    def ring_step(t):
        for way in range(2):
            slot = chip_slot(odd - 2 * t - 1) if way == 0 else chip_slot(odd + 1 + 2 * t)
            for k in range(SUBS):
                leaf_out[way, t, k] = local_sum(slot, k).astype(BF16)
            leaf(way, t).start()

        def pass_on(way, k, slot):
            if k == 0:
                guarded(t > 0, lambda: leaf(way, t - 1).wait_recv())
            guarded(t > way, lambda: hop(way, t - 1, k).wait_recv())
            acc_out[way, t, k] = (
                acc_in[way, t, k].astype(F32) + leaf_in[way, t, k].astype(F32) + local_sum(slot, k)
            ).astype(BF16)
            hop(way, t, k).start()

        for k in range(SUBS):
            pass_on(0, k, chip_slot(odd - 2 * t))
            guarded(t > 0, lambda: pass_on(1, k, chip_slot(odd + 2 * t)))

    send_rows(0)
    for_peers(lambda j: prob_copy(j).start())
    pick_rows(1)
    send_rows(1)
    load_stored.wait()
    quarter = rows // 4
    gates(0, quarter)
    gates(1, quarter)
    pick_rows(2)
    send_rows(2)
    gates(2, quarter)
    gates(3, quarter)
    pick_rows(3)
    pick_rows(4)
    row_at = lax.broadcasted_iota(jnp.int32, (rows, OWNERS * PAD), 0).astype(F32)
    padded_at = row_at + float(PAD - cap) * jnp.floor((row_at + 0.5) * (1.0 / cap))
    compact[...] = jnp.where(
        lax.broadcasted_iota(jnp.int32, (rows, OWNERS * PAD), 1).astype(F32) == padded_at, 1.0, 0.0
    ).astype(BF16)
    acc_in[0, 0] = jnp.zeros(acc_in.shape[2:], BF16)
    acc_in[1, 1] = jnp.zeros(acc_in.shape[2:], BF16)
    leaf_in[0, 0] = jnp.zeros(leaf_in.shape[2:], BF16)
    send_rows(3)
    for_peers(lambda j: prob_copy(j).wait_recv())
    prob_col[...] = jnp.dot(
        compact[...], prob_in[...].reshape(OWNERS * PAD, HALF), preferred_element_type=F32
    )
    back[...] = jnp.zeros_like(back)

    def early(i, carry):
        stage_e(i)
        return carry

    lax.fori_loop(0, 3, early, 0)
    send_rows(4)
    sib_copy(0).wait_recv()

    def turn(t, carry):
        sib_copy(t + 1).wait_recv()
        ring_step(t)

        @pl.when(t < 3)
        def _():
            pick_rows(t + 5)
            send_rows(t + 5)

        @pl.when(t < 5)
        def _():
            stage_e(t + 3)

        add_back(t)
        return carry

    lax.fori_loop(0, 6, turn, 0)
    add_back(6)
    sib_copy(7).wait_recv()
    ring_step(6)
    add_back(7)

    products = jnp.sum(hidden[...].astype(F32) * back[...], axis=1, keepdims=True)
    row_at = lax.broadcasted_iota(jnp.int32, (rows, HALF), 0).astype(F32)
    row_slot = row_at - float(cap) * jnp.floor((row_at + 0.5) * (1.0 / cap))
    lane_at = lax.broadcasted_iota(jnp.int32, (rows, HALF), 1).astype(F32)
    spread = jnp.where(lane_at == row_slot, jnp.broadcast_to(products, (rows, HALF)), 0.0)
    src_at = jnp.floor((lax.broadcasted_iota(jnp.int32, (OWNERS, rows), 1).astype(F32) + 0.5) * (1.0 / cap))
    gather = jnp.where(src_at == lax.broadcasted_iota(jnp.int32, (OWNERS, rows), 0).astype(F32), 1.0, 0.0)
    by_source = jnp.dot(gather, spread, preferred_element_type=F32, precision=lax.Precision.HIGHEST)
    for s in range(OWNERS):
        prod_out[s] = jnp.broadcast_to(by_source[s : s + 1], (8, HALF))
    prod_in[me] = prod_out[me]
    for_peers(lambda j: prod_copy(j).start())

    def finish_rows(b, size):
        at = pl.ds(b * size, size)
        scale = jnp.concatenate([prob_col[at, :]] * (hid_n // HALF), axis=1)
        grad = scale * back[at, :]
        pre[at, :hid_n] = (grad * d_gate[at, :]).astype(BF16)
        pre[at, hid_n:] = (grad * d_up[at, :]).astype(BF16)

    def store_pre(b, size):
        at = pl.ds(b * size, size)
        return pltpu.make_async_copy(pre.at[at], pre_hbm.at[at], sem_pre.at[b])

    half_rows = rows // 2
    finish_rows(0, half_rows)
    store_pre(0, half_rows).start()
    ring_step(7)
    finish_rows(1, half_rows)
    store_pre(1, half_rows).start()

    for_peers(lambda j: prod_copy(j).wait_recv())
    sub16 = lax.broadcasted_iota(jnp.int32, (OWNERS, HALF), 0)
    by_owner = jnp.zeros((OWNERS, HALF), F32)
    for e in range(OWNERS):
        by_owner = jnp.where(sub16 == e, jnp.broadcast_to(prod_in[e, 0:1, :], (OWNERS, HALF)), by_owner)
    by_slot = jnp.concatenate([by_owner, jnp.zeros((HALF - OWNERS, HALF), F32)], axis=0).T
    result = jnp.zeros((top, tok), F32)
    for e in range(OWNERS):
        match = jnp.broadcast_to(slots[e : e + 1], (PAD, tok)) == slot_at
        value = jnp.sum(
            jnp.where(match, jnp.broadcast_to(by_slot[0:PAD, e : e + 1], (PAD, tok)), 0.0), axis=0, keepdims=True
        )
        result = jnp.where(ids == e, jnp.broadcast_to(value, (top, tok)), result)
    gprobs_ref[...] = result

    def drain(i, carry):
        for_peers(lambda j: row_copy(i, j).wait_send())
        sib_copy(i).wait_send()
        return carry

    lax.fori_loop(0, CHUNKS, drain, 0)
    for_peers(lambda j: prob_copy(j).wait_send())
    for_peers(lambda j: prod_copy(j).wait_send())
    for way in range(2):

        def drain_ring(t, carry):
            for k in range(SUBS):
                hop(way, t, k).wait_send()
            return carry

        def drain_leaf(t, carry):
            leaf(way, t).wait_send()
            return carry

        lax.fori_loop(way, STEPS - 1, drain_ring, 0)
        lax.fori_loop(0, STEPS - 1, drain_leaf, 0)

    own = chip_slot(odd - REACH)
    piece = SHARE // SUBS
    for way in range(2):
        leaf(way, STEPS - 1).wait_recv()
    for k in range(SUBS):
        for way in range(2):
            hop(way, STEPS - 1, k).wait_recv()
        down_ref[0, k * piece : (k + 1) * piece, :] = (
            (acc_in[0, STEPS, k].astype(F32) + acc_in[1, STEPS, k].astype(F32))
            + (leaf_in[0, STEPS, k].astype(F32) + leaf_in[1, STEPS, k].astype(F32))
            + local_sum(own, k)
        )

    for way in range(2):
        leaf(way, STEPS - 1).wait_send()
        for k in range(SUBS):
            hop(way, STEPS - 1, k).wait_send()
    store_pre(0, half_rows).wait()
    store_pre(1, half_rows).wait()


def local(out_grad, probs, expert_ids, saved_pre, down_weight):
    top, tok = expert_ids.shape[1], expert_ids.shape[0]
    rows, pre_n = saved_pre.shape
    hid_n = pre_n // 2
    piece = SHARE // SUBS
    dma = pltpu.SemaphoreType.DMA
    scratch = [
        pltpu.VMEM((CHUNKS, tok, WIDTH), BF16),
        pltpu.VMEM((CHUNKS, WIDTH, hid_n), BF16),
        pltpu.VMEM((rows, pre_n), BF16),
        pltpu.VMEM((rows, hid_n), BF16),
        pltpu.VMEM((rows, hid_n), F32),
        pltpu.VMEM((rows, hid_n), F32),
        pltpu.VMEM((rows, hid_n), F32),
        pltpu.VMEM((CHUNKS, rows, WIDTH), BF16),
        pltpu.VMEM((rows, pre_n), BF16),
        pltpu.VMEM((OWNERS * PAD, tok), BF16),
        pltpu.VMEM((CHUNKS, OWNERS, PAD, WIDTH), BF16),
        pltpu.VMEM((CHUNKS, OWNERS, PAD, WIDTH), BF16),
        pltpu.VMEM((OWNERS, PAD, HALF), BF16),
        pltpu.VMEM((OWNERS, PAD, HALF), BF16),
        pltpu.VMEM((rows, OWNERS * PAD), BF16),
        pltpu.VMEM((rows, HALF), F32),
        pltpu.VMEM((OWNERS, 8, HALF), F32),
        pltpu.VMEM((OWNERS, 8, HALF), F32),
        pltpu.VMEM((CHIPS, 2, SUBS, piece, hid_n), BF16),
        pltpu.VMEM((CHIPS, SUBS, piece, hid_n), BF16),
        pltpu.VMEM((2, STEPS, SUBS, piece, hid_n), BF16),
        pltpu.VMEM((2, STEPS + 1, SUBS, piece, hid_n), BF16),
        pltpu.VMEM((2, STEPS, SUBS, piece, hid_n), BF16),
        pltpu.VMEM((2, STEPS + 1, SUBS, piece, hid_n), BF16),
        dma((CHUNKS, 2)), dma((CHUNKS, 2)), dma, dma((2,)),
        dma((CHUNKS, OWNERS)), dma((CHUNKS, OWNERS)),
        dma((OWNERS,)), dma((OWNERS,)), dma((OWNERS,)), dma((OWNERS,)),
        dma((CHUNKS,)), dma((CHUNKS,)),
        dma((2, STEPS, SUBS)), dma((2, STEPS, SUBS)), dma((2, STEPS)), dma((2, STEPS)),
    ]
    hbm = pl.BlockSpec(memory_space=pl.ANY)
    vmem = pl.BlockSpec(memory_space=pltpu.VMEM)
    down, pre, gprobs = pl.pallas_call(
        kernel,
        out_shape=(
            jax.ShapeDtypeStruct((1, SHARE, hid_n), F32),
            jax.ShapeDtypeStruct((rows, pre_n), BF16),
            jax.ShapeDtypeStruct((top, tok), F32),
        ),
        in_specs=[hbm, vmem, vmem, hbm, hbm],
        out_specs=(vmem, hbm, vmem),
        scratch_shapes=scratch,
        compiler_params=pltpu.CompilerParams(
            collective_id=0, has_side_effects=True, vmem_limit_bytes=56 * 1024 * 1024
        ),
    )(out_grad, probs.T, expert_ids.T, saved_pre, down_weight)
    return down, pre, gprobs.T


def solution(mesh):
    in_specs = (
        P(("dp", "expert"), None),
        P(("dp", "expert"), None),
        P(("dp", "expert"), None),
        P(("dp", "expert"), None),
        P("expert", None, None),
    )
    out_specs = (P("expert", "dp", None), P(("dp", "expert"), None), P(("dp", "expert"), None))
    return jax.shard_map(local, mesh=mesh, in_specs=in_specs, out_specs=out_specs, check_vma=False)
```

time: 106 us -> 81.8 us (0.77)
  Pallas kernels: 96.6 us -> 76.3 us
  local copies, waits for them, and re-layouts: 8.18 us -> 4.64 us
    pallas_call x1, Pallas kernels: 96.6 us -> 76.3 us  [local(): pl.pallas_call(kernel, out_shape=(jax.ShapeDtypeStruct((1, SHARE, hid_n),...]
    unnamed x4 -> x5, local copies, waits for them, and re-layouts: 6.78 us -> 4.64 us
    pallas_call x1 -> x0, local copies, waits for them, and re-layouts: 1.4 us -> none  [local(): pl.pallas_call(kernel, out_shape=(jax.ShapeDtypeStruct((1, SHARE, hid_n),...]
where the time goes in v2:
time: 81.8 us; the launch traced here: 81.5 us
  Pallas kernels  76.3 us (93%)
  local copies, waits for them, and re-layouts  4.64 us (6%)
    pallas_call x1, Pallas kernels, local(): pl.pallas_call(kernel, out_shape=(jax.ShapeDtypeStruct((1, SHARE, hid_n),...  76.3 us
    unnamed x5, local copies, waits for them, and re-layouts  4.64 us

profile of v2, /device:TPU:24, one launch (start us, length us, event | category | flops | bytes accessed | tf_op | source)
XLA Modules:
  0.0 81.5 jit_solution(13043601951357788634)
XLA Ops:
  0.6 76.3 %shard_map.76 = (f32[1,32,768]{2,1,0:T(8,128)}, bf16[448,1536]{1,0:T(8,128)(2,1)}, f32[8,48]{1,0:T(8,128)}) custom-call(bf16[48,2048]{1,0:T(8,128)(2,1)} %grad_hbm.1, bf16[8,48]{1,0:T(8,128)(2,1)} %bitcast.5, s32[8,48]{1,0:T(8,128)} %bitcast.3, bf16[448,1536]{1,0:T(8,128)(2,1)} %stored_hbm.1, bf16[1,2048,768]{2,1,0:T(8,128)(2,1)} %weight_hbm.1), custom_call_target="tpu_custom_call" | custom-call | tf_op jit(solution)/shard_map/pallas_call | solution.py:428
  76.9 1.5 %copy.11 = f32[1,32,768]{2,1,0:T(8,128)} copy(f32[1,32,768]{2,1,0:T(8,128)} %get-tuple-element.12) | data formatting | bytes 196608
  78.4 0.0 copy-start
  78.4 2.5 %copy.12 = bf16[448,1536]{1,0:T(8,128)(2,1)} copy(bf16[448,1536]{1,0:T(8,128)(2,1)} %get-tuple-element.13) | data formatting | bytes 2752512
  80.9 0.0 copy-done
  80.9 0.6 copy.13
Async XLA Ops:
  78.4 2.5 %copy-start = (f32[8,48]{1,0:T(8,128)S(1)}, f32[8,48]{1,0:T(8,128)}, u32[]{:S(2)}) copy-start(f32[8,48]{1,0:T(8,128)} %get-tuple-element.8) | copy-start | bytes 4612

commit v3 on v2

--- a/solution.py
+++ b/solution.py
@@ -384,6 +384,27 @@
             hop(way, STEPS - 1, k).wait_send()
     store_pre(0, half_rows).wait()
     store_pre(1, half_rows).wait()
+
+
+PIECES = 7
+
+
+def hand_on(down_in, pre_in, gprobs_in, down_out, pre_out, gprobs_out, down_buf, pre_buf, gprobs_buf, sems_in, sems_out):
+    size = pre_in.shape[0] // PIECES
+    trips = [
+        (pre_in.at[pl.ds(b * size, size)], pre_buf.at[pl.ds(b * size, size)], pre_out.at[pl.ds(b * size, size)])
+        for b in range(PIECES)
+    ]
+    trips += [(down_in, down_buf, down_out), (gprobs_in, gprobs_buf, gprobs_out)]
+    reads = [pltpu.make_async_copy(src, buf, sems_in.at[n]) for n, (src, buf, _) in enumerate(trips)]
+    writes = [pltpu.make_async_copy(buf, dst, sems_out.at[n]) for n, (_, buf, dst) in enumerate(trips)]
+    for read in reads:
+        read.start()
+    for read, write in zip(reads, writes):
+        read.wait()
+        write.start()
+    for write in writes:
+        write.wait()
 
 
 def local(out_grad, probs, expert_ids, saved_pre, down_weight):
@@ -439,6 +460,15 @@
             collective_id=0, has_side_effects=True, vmem_limit_bytes=56 * 1024 * 1024
         ),
     )(out_grad, probs.T, expert_ids.T, saved_pre, down_weight)
+    down, pre, gprobs = pl.pallas_call(
+        hand_on,
+        out_shape=tuple(jax.ShapeDtypeStruct(a.shape, a.dtype) for a in (down, pre, gprobs)),
+        in_specs=[hbm] * 3,
+        out_specs=(hbm, hbm, hbm),
+        scratch_shapes=[pltpu.VMEM(a.shape, a.dtype) for a in (down, pre, gprobs)]
+        + [dma((PIECES + 2,)), dma((PIECES + 2,))],
+        compiler_params=pltpu.CompilerParams(vmem_limit_bytes=56 * 1024 * 1024),
+    )(down, pre, gprobs)
     return down, pre, gprobs.T
 
 

time: 81.8 us -> 79.4 us (0.971)
  local copies, waits for them, and re-layouts: 4.64 us -> 0 us
  Pallas kernels: 76.3 us -> 78.5 us
    unnamed x5 -> x0, local copies, waits for them, and re-layouts: 4.64 us -> none
    pallas_call x0 -> x1, Pallas kernels: none -> 2.28 us  [local(): pl.pallas_call(hand_on, out_shape=tuple((jax.ShapeDtypeStruct(a.shape, a....]
where the time goes in v3:
time: 79.4 us; the launch traced here: 79.2 us
  Pallas kernels  78.5 us (99%)
    pallas_call x1, Pallas kernels, local(): pl.pallas_call(kernel, out_shape=(jax.ShapeDtypeStruct((1, SHARE, hid_n),...  76.3 us
    pallas_call x1, Pallas kernels, local(): pl.pallas_call(hand_on, out_shape=tuple((jax.ShapeDtypeStruct(a.shape, a....  2.28 us

profile of v3, /device:TPU:24, one launch (start us, length us, event | category | flops | bytes accessed | tf_op | source)
XLA Modules:
  0.0 79.2 jit_solution(15306327118326774305)
XLA Ops:
  0.6 76.3 %shard_map.76 = (f32[1,32,768]{2,1,0:T(8,128)}, bf16[448,1536]{1,0:T(8,128)(2,1)}, f32[8,48]{1,0:T(8,128)}) custom-call(bf16[48,2048]{1,0:T(8,128)(2,1)} %grad_hbm.1, bf16[8,48]{1,0:T(8,128)(2,1)} %bitcast.4, s32[8,48]{1,0:T(8,128)} %bitcast.3, bf16[448,1536]{1,0:T(8,128)(2,1)} %stored_hbm.1, bf16[1,2048,768]{2,1,0:T(8,128)(2,1)} %weight_hbm.1), custom_call_target="tpu_custom_call" | custom-call | tf_op jit(solution)/shard_map/pallas_call | solution.py:449
  76.9 2.3 %shard_map.77 = (f32[1,32,768]{2,1,0:T(8,128)}, bf16[448,1536]{1,0:T(8,128)(2,1)}, f32[8,48]{1,0:T(8,128)}) custom-call(f32[1,32,768]{2,1,0:T(8,128)} %get-tuple-element.9.down_in, bf16[448,1536]{1,0:T(8,128)(2,1)} %get-tuple-element.10.pre_in, f32[8,48]{1,0:T(8,128)} %get-tuple-element.11.gprobs_in), custom_call_target="tpu_custom_call" | custom-call | tf_op jit(solution)/shard_map/pallas_call | solution.py:463

commit v4 on v3

--- a/solution.py
+++ b/solution.py
@@ -183,9 +183,12 @@
         sib_copy(i).start()
 
     def add_back(i):
-        load_w(i, 0).wait()
-        load_w(i, 1).wait()
-        back[...] += jnp.dot(routed_all[i], w[i], preferred_element_type=F32)
+        for n in range(2):
+            load_w(i + n, 0).wait()
+            load_w(i + n, 1).wait()
+        back[...] += jnp.dot(routed_all[i], w[i], preferred_element_type=F32) + jnp.dot(
+            routed_all[i + 1], w[i + 1], preferred_element_type=F32
+        )
 
     def chip_slot(off):
         at = off + REACH
@@ -288,14 +291,16 @@
         def _():
             stage_e(t + 3)
 
-        add_back(t)
+        @pl.when(rem(t, 2) == 1)
+        def _():
+            add_back(t - 1)
+
         return carry
 
     lax.fori_loop(0, 6, turn, 0)
-    add_back(6)
     sib_copy(7).wait_recv()
     ring_step(6)
-    add_back(7)
+    add_back(6)
 
     products = jnp.sum(hidden[...].astype(F32) * back[...], axis=1, keepdims=True)
     row_at = lax.broadcasted_iota(jnp.int32, (rows, HALF), 0).astype(F32)

time: 79.4 us -> 79.4 us (level)
  no operation moved by 1% of the time
where the time goes in v4:
time: 79.4 us; the launch traced here: 79.2 us
  Pallas kernels  78.5 us (99%)
    pallas_call x1, Pallas kernels, local(): pl.pallas_call(kernel, out_shape=(jax.ShapeDtypeStruct((1, SHARE, hid_n),...  76.3 us
    pallas_call x1, Pallas kernels, local(): pl.pallas_call(hand_on, out_shape=tuple((jax.ShapeDtypeStruct(a.shape, a....  2.28 us

profile of v4, /device:TPU:24, one launch (start us, length us, event | category | flops | bytes accessed | tf_op | source)
XLA Modules:
  0.0 79.2 jit_solution(3022495351304398560)
XLA Ops:
  0.6 76.3 %shard_map.76 = (f32[1,32,768]{2,1,0:T(8,128)}, bf16[448,1536]{1,0:T(8,128)(2,1)}, f32[8,48]{1,0:T(8,128)}) custom-call(bf16[48,2048]{1,0:T(8,128)(2,1)} %grad_hbm.1, bf16[8,48]{1,0:T(8,128)(2,1)} %bitcast.4, s32[8,48]{1,0:T(8,128)} %bitcast.3, bf16[448,1536]{1,0:T(8,128)(2,1)} %stored_hbm.1, bf16[1,2048,768]{2,1,0:T(8,128)(2,1)} %weight_hbm.1), custom_call_target="tpu_custom_call" | custom-call | tf_op jit(solution)/shard_map/pallas_call | solution.py:454
  76.9 2.3 %shard_map.77 = (f32[1,32,768]{2,1,0:T(8,128)}, bf16[448,1536]{1,0:T(8,128)(2,1)}, f32[8,48]{1,0:T(8,128)}) custom-call(f32[1,32,768]{2,1,0:T(8,128)} %get-tuple-element.9.down_in, bf16[448,1536]{1,0:T(8,128)(2,1)} %get-tuple-element.10.pre_in, f32[8,48]{1,0:T(8,128)} %get-tuple-element.11.gprobs_in), custom_call_target="tpu_custom_call" | custom-call | tf_op jit(solution)/shard_map/pallas_call | solution.py:468
